TPU v7x, 128 devices: a whole 4x4x4 slice. The times are simulated.
128 devices in a mesh: arc: 8 (over x, core), par: 16 (over y, z).
Axes of the slice: x: 4, y: 4, z: 4, core: 2. Of those that a mesh axis runs over, the one named last changes fastest.
Arguments:
- observations: float32 [2048, 65536], P('arc', 'par'), may hold values from -18 to 18
- arc_mask: int32 [16, 512], P('arc', 'par'), may hold values 0 or 1
- panel_owner: int32 [2], replicated, may hold values from 0 to 255, as said below
Outputs:
- info_rows: float32 [512, 65536], P('arc', 'par')
Inputs may be any that keep to these rules, and one draw needn't show every extreme that they name: `panel_owner`: two different panel indices below 256; one of the two is always the last panel.
All inputs are finite; a program needn't handle non-finite values. No bound on the sum of `arc_mask` on one device may be relied on, other than what follows from the above.
Results may differ from a plain program's by a relative error of at most 0.002.
Values sent between devices are 32-bit elements; how exact they have to be, the bound alone decides.
A program may use at most 64 MiB of HBM per device.

v0:
```python
import math
import jax
import jax.numpy as jnp
from jax import lax
from jax.sharding import PartitionSpec as P

PANEL = 256
BLK = 128


def spread(array, axis, root):
    mine = lax.axis_index(axis) == root
    return lax.psum(jnp.where(mine, array, jnp.zeros_like(array)), axis)


def matmul_high(left, right):
    return jnp.dot(left, right, precision=lax.Precision.HIGHEST, preferred_element_type=jnp.float32)


def inner_high(left, right):
    return lax.dot_general(
        left,
        right,
        (((0,), (0,)), ((), ())),
        precision=lax.Precision.HIGHEST,
        preferred_element_type=jnp.float32,
    )


def cholesky_loop(gram):
    order = gram.shape[0]
    positions = lax.broadcasted_iota(jnp.int32, (order, 1), 0)

    def one_column(column, lower):
        lower_row = lax.dynamic_slice_in_dim(lower, column, 1, 0)
        gram_col = lax.dynamic_slice_in_dim(gram, column, 1, 1)
        values = gram_col - matmul_high(lower, lower_row.T)
        pivot = lax.dynamic_slice_in_dim(values, column, 1, 0)
        scaled = jnp.where(positions >= column, values / jnp.sqrt(pivot), 0.0)
        return lax.dynamic_update_slice_in_dim(lower, scaled, column, 1)

    return lax.fori_loop(0, order, one_column, jnp.zeros_like(gram))


def lower_inverse(lower):
    order = lower.shape[0]
    columns = lax.broadcasted_iota(jnp.int32, (1, order), 1)

    def one_row(index, inverse):
        lower_row = lax.dynamic_slice_in_dim(lower, index, 1, 0)
        diag_entry = lax.dynamic_slice_in_dim(lower_row, index, 1, 1)
        unit_row = jnp.where(columns == index, 1.0, 0.0).astype(jnp.float32)
        new_row = (unit_row - matmul_high(lower_row, inverse)) / diag_entry
        return lax.dynamic_update_slice_in_dim(inverse, new_row, index, 0)

    return lax.fori_loop(0, order, one_row, jnp.zeros_like(lower))


def share_panel(design, panel_index):
    col_count = design.shape[1]
    col_start = panel_index * PANEL
    owner_root = col_start // col_count
    offset = col_start - owner_root * col_count
    local_cols = lax.dynamic_slice_in_dim(design, offset, PANEL, 1)
    return spread(local_cols, "par", owner_root)


def own_rows(stacked):
    arc_count = lax.axis_size("arc")
    row_share = stacked.shape[0] // arc_count
    row_start = lax.axis_index("arc") * row_share
    return lax.dynamic_slice_in_dim(stacked, row_start, row_share, 0)


def shards(observations, arc_mask, panel_owner):
    row_count, col_count = observations.shape
    row_blocks, col_blocks = arc_mask.shape
    total_rows = row_count * lax.axis_size("arc")
    shaped = observations.reshape(row_blocks, BLK, col_blocks, BLK)
    masked = shaped * arc_mask.astype(jnp.float32)[:, None, :, None]
    design = masked.reshape(row_count, col_count) / math.sqrt(total_rows)
    rows_out = []
    for panel_turn in range(2):
        panel_cols = share_panel(design, panel_owner[panel_turn])
        gram_block, cross_sums = lax.psum(
            (inner_high(panel_cols, panel_cols), inner_high(panel_cols, design)), "arc"
        )
        inverse = lower_inverse(cholesky_loop(gram_block))
        factor = matmul_high(inverse, cross_sums)
        rows_out.append(factor)
        if panel_turn == 0:
            coefficients = matmul_high(inverse.T, factor)
            design = design - matmul_high(panel_cols, coefficients)
    return own_rows(jnp.concatenate(rows_out, 0))


def solution(mesh):
    return jax.shard_map(
        shards,
        mesh=mesh,
        in_specs=(P("arc", "par"), P("arc", "par"), P()),
        out_specs=P("arc", "par"),
        check_vma=False,
    )
```

profile of v0, /device:TPU:0, one launch (start us, length us, event | category | flops | bytes accessed | tf_op | source)
XLA Modules:
  0.0 2377.6 jit_solution(8174050808208383253)
XLA Ops:
  6.5 1.4 fusion.28
  8.6 0.7 convert_element_type.3
  9.9 1.6 copy-done.5
  11.5 4.1 fusion.24
  15.6 2.0 copy-done
  17.5 0.7 dynamic-slice_select_fusion.1
  18.3 87.0 %all-reduce.7.cloned.1.call-done = f32[256,256]{1,0:T(8,128)} async-done(((f32[256,256]{1,0:T(8,128)}), f32[256,256]{1,0:T(8,128)}) %all-reduce.7.cloned.1.call-update) | async-done | bytes 262160 | tf_op jit(solution)/shard_map/psum | solution.py:13
  105.4 8.0 fusion.30
  113.4 1.3 fusion.29
  115.6 72.0 %all-reduce.13.cloned.1.call-done = (f32[256,256]{1,0:T(8,128)}, f32[256,4096]{1,0:T(8,128)}) async-done(((f32[256,256]{1,0:T(8,128)}, f32[256,4096]{1,0:T(8,128)}), (f32[256,256]{1,0:T(8,128)}, f32[256,4096]{1,0:T(8,128)})) %all-reduce.13.cloned.1.call-update) | async-done | bytes 4456464 | tf_op jit(solution)/shard_map/psum | solution.py:85
  187.5 1.1 copy.11
  188.7 602.1 %while.62 = (s32[]{:T(128)}, f32[256,256]{1,0:T(8,128)S(1)}, f32[256,256]{0,1:T(8,128)S(1)}, s32[]{:T(128)}, s32[]{:T(128)}) while((s32[]{:T(128)}, f32[256,256]{1,0:T(8,128)S(1)}, f32[256,256]{0,1:T(8,128)S(1)}, s32[]{:T(128)}, s32[]{:T(128)}) %tuple.138), condition=%wide.region_3.4_spmd.clone, body=%wide.region_2.3_spmd.clone.sunk | while | flops 787458 | bytes 272469 | solution.py:42
  196.5 0.7 compare_select_fusion.8
  201.2 0.7 compare_select_fusion.8
  208.3 0.7 compare_select_fusion.8
  213.0 0.7 compare_select_fusion.8
  224.7 0.7 compare_select_fusion.8
  229.4 0.7 compare_select_fusion.8
  241.2 0.7 compare_select_fusion.8
  245.9 0.7 compare_select_fusion.8
  253.0 0.7 compare_select_fusion.8
  257.7 0.7 compare_select_fusion.8
  269.4 0.7 compare_select_fusion.8
  274.1 0.7 compare_select_fusion.8
  285.9 0.7 compare_select_fusion.8
  290.6 0.7 compare_select_fusion.8
  297.7 0.7 compare_select_fusion.8
  302.4 0.7 compare_select_fusion.8
  314.1 0.7 compare_select_fusion.8
  318.8 0.7 compare_select_fusion.8
  330.6 0.7 compare_select_fusion.8
  335.3 0.7 compare_select_fusion.8
  342.4 0.7 compare_select_fusion.8
  790.8 393.8 %while.63 = (s32[]{:T(128)}, f32[256,256]{1,0:T(8,128)S(1)}, f32[256,256]{1,0:T(8,128)S(1)}, s32[]{:T(128)}, s32[]{:T(128)}, /*index=5*/s32[]{:T(128)}) while((s32[]{:T(128)}, f32[256,256]{1,0:T(8,128)S(1)}, f32[256,256]{1,0:T(8,128)S(1)}, s32[]{:T(128)}, s32[]{:T(128)}, /*index=5*/s32[]{:T(128)}) %tuple.141), condition=%wide.region_5.6_spmd.clone, body=%wide.region_4.5_spmd.clone.sunk | while | flops 787459 | bytes 270449 | solution.py:56
  1184.6 5.4 fusion.31
  1190.0 3.8 fusion.32
  1193.9 3.8 convolution_subtract_fusion
  1197.7 2.0 copy-done.4
  1199.6 0.7 dynamic-slice_select_fusion
  1200.6 84.5 %all-reduce.9.cloned.1.call-done = f32[256,256]{1,0:T(8,128)} async-done(((f32[256,256]{1,0:T(8,128)}), f32[256,256]{1,0:T(8,128)}) %all-reduce.9.cloned.1.call-update) | async-done | bytes 262160 | tf_op jit(solution)/shard_map/psum | solution.py:13
  1285.1 8.0 fusion.34
  1293.1 1.3 fusion.33
  1294.5 72.8 %all-reduce.11.cloned.1.call-done = (f32[256,256]{1,0:T(8,128)}, f32[256,4096]{1,0:T(8,128)}) async-done(((f32[256,256]{1,0:T(8,128)}, f32[256,4096]{1,0:T(8,128)}), (f32[256,256]{1,0:T(8,128)}, f32[256,4096]{1,0:T(8,128)})) %all-reduce.11.cloned.1.call-update) | async-done | bytes 4456464 | tf_op jit(solution)/shard_map/psum | solution.py:85
  1367.3 1.1 copy.12
  1368.4 602.1 %while.64 = (s32[]{:T(128)}, f32[256,256]{1,0:T(8,128)S(1)}, f32[256,256]{0,1:T(8,128)S(1)}, s32[]{:T(128)}, s32[]{:T(128)}) while((s32[]{:T(128)}, f32[256,256]{1,0:T(8,128)S(1)}, f32[256,256]{0,1:T(8,128)S(1)}, s32[]{:T(128)}, s32[]{:T(128)}) %tuple.144), condition=%wide.region_10.11_spmd.clone, body=%wide.region_9.10_spmd.clone.sunk | while | flops 787458 | bytes 272469 | solution.py:42
  1970.5 393.8 %while.65 = (s32[]{:T(128)}, f32[256,256]{1,0:T(8,128)S(1)}, f32[256,256]{1,0:T(8,128)S(1)}, s32[]{:T(128)}, s32[]{:T(128)}, /*index=5*/s32[]{:T(128)}) while((s32[]{:T(128)}, f32[256,256]{1,0:T(8,128)S(1)}, f32[256,256]{1,0:T(8,128)S(1)}, s32[]{:T(128)}, s32[]{:T(128)}, /*index=5*/s32[]{:T(128)}) %tuple.147), condition=%wide.region_12.13_spmd.clone, body=%wide.region_11.12_spmd.clone.sunk | while | flops 787459 | bytes 270449 | solution.py:56
  2364.4 5.6 fusion.35
  2370.0 1.1 fusion.25
  (5125 shorter events, 1945.0 us)
Async XLA Ops:
  6.5 98.8 %all-reduce.7.cloned.1.call-start = ((), (), s32[]{:S(2)}) async-start(), calls=%async_computation | async-start | bytes 524288 | tf_op jit(solution)/shard_map/psum | solution.py:13
  9.3 2.2 copy-start.5
  15.6 2.0 copy-start
  18.3 169.3 %all-reduce.13.cloned.1.call-start = ((), (), s32[]{:S(2)}) async-start(), calls=%async_computation.3 | async-start | bytes 8912896 | tf_op jit(solution)/shard_map/psum | solution.py:85
  105.3 8.0 copy-start.6
  114.7 1170.4 %all-reduce.9.cloned.1.call-start = ((), (), s32[]{:S(2)}) async-start(), calls=%async_computation.1 | async-start | bytes 524288 | tf_op jit(solution)/shard_map/psum | solution.py:13
  1190.0 3.8 copy-start.2
  1190.0 3.8 copy-start.1
  1197.7 2.0 copy-start.4
  1200.4 166.9 %all-reduce.11.cloned.1.call-start = ((), (), s32[]{:S(2)}) async-start(), calls=%async_computation.2 | async-start | bytes 8912896 | tf_op jit(solution)/shard_map/psum | solution.py:85
  1285.1 8.0 copy-start.7
  2364.4 5.6 copy-start.3
Sparse Core Ops, SparseCore 0:
  18.4 86.9 all-reduce.6
  114.8 72.6 all-reduce.12
  1200.5 84.5 all-reduce.8
  1294.6 72.6 all-reduce.10
where the time goes:
time: 2390 us; the launch traced here: 2380 us
  local copies, waits for them, and re-layouts  1070 us (45%)
  other arithmetic  675 us (28%)
  waiting for transfers between devices  316 us (13%)
  matrix products  270 us (11%)
  loops' own time  34.5 us (1%)
    select_n x512, other arithmetic, one_column(): scaled = jnp.where(positions >= column, values / jnp.sqrt(pivot), 0.0)  333 us
    sqrt x512, local copies, waits for them, and re-layouts, one_column(): scaled = jnp.where(positions >= column, values / jnp.sqrt(pivot), 0.0)  332 us
    div x512, other arithmetic, one_row(): new_row = (unit_row - matmul_high(lower_row, inverse)) / diag_entry  332 us
    dynamic_slice x512, local copies, waits for them, and re-layouts, one_row(): diag_entry = lax.dynamic_slice_in_dim(lower_row, index, 1, 1)  321 us
    dynamic_update_slice x512, local copies, waits for them, and re-layouts, one_column(): return lax.dynamic_update_slice_in_dim(lower, scaled, column, 1)  314 us
    dot_general x1028, matrix products, matmul_high(): jnp.dot(left, right, precision=lax.Precision.HIGHEST, preferred_element_t...  251 us
    psum x2, waiting for transfers between devices, spread(): return lax.psum(jnp.where(mine, array, jnp.zeros_like(array)), axis)  171 us
    psum x2, waiting for transfers between devices, shards(): lax.psum((inner_high(panel_cols, panel_cols), inner_high(panel_cols, desi...  145 us

commit v1 on v0

--- a/solution.py
+++ b/solution.py
@@ -10,7 +10,7 @@
 
 def spread(array, axis, root):
     mine = lax.axis_index(axis) == root
-    return lax.psum(jnp.where(mine, array, jnp.zeros_like(array)), axis)
+    return jnp.sum(lax.all_gather(jnp.where(mine, array, jnp.zeros_like(array)), axis), axis=0)
 
 
 def matmul_high(left, right):

time: 2390 us -> 2330 us (0.975)
  waiting for transfers between devices: 316 us -> 252 us
    psum x2 -> x0, waiting for transfers between devices: 171 us -> none  [spread(): return lax.psum(jnp.where(mine, array, jnp.zeros_like(array)), axis)]
    all_gather x0 -> x2, waiting for transfers between devices: none -> 106 us  [spread(): lax.all_gather(jnp.where(mine, array, jnp.zeros_like(array)), axis)]
where the time goes in v1:
time: 2330 us; the launch traced here: 2320 us
  local copies, waits for them, and re-layouts  1070 us (46%)
  other arithmetic  680 us (29%)
  matrix products  270 us (12%)
  waiting for transfers between devices  252 us (11%)
  loops' own time  34.5 us (1%)
    select_n x512, other arithmetic, one_column(): scaled = jnp.where(positions >= column, values / jnp.sqrt(pivot), 0.0)  333 us
    sqrt x512, local copies, waits for them, and re-layouts, one_column(): scaled = jnp.where(positions >= column, values / jnp.sqrt(pivot), 0.0)  332 us
    div x512, other arithmetic, one_row(): new_row = (unit_row - matmul_high(lower_row, inverse)) / diag_entry  332 us
    dynamic_slice x512, local copies, waits for them, and re-layouts, one_row(): diag_entry = lax.dynamic_slice_in_dim(lower_row, index, 1, 1)  321 us
    dynamic_update_slice x512, local copies, waits for them, and re-layouts, one_column(): return lax.dynamic_update_slice_in_dim(lower, scaled, column, 1)  314 us
    dot_general x1028, matrix products, matmul_high(): jnp.dot(left, right, precision=lax.Precision.HIGHEST, preferred_element_t...  251 us
    psum x2, waiting for transfers between devices, shards(): lax.psum((inner_high(panel_cols, panel_cols), inner_high(panel_cols, desi...  146 us
    all_gather x2, waiting for transfers between devices, spread(): lax.all_gather(jnp.where(mine, array, jnp.zeros_like(array)), axis)  106 us

profile of v1, /device:TPU:0, one launch (start us, length us, event | category | flops | bytes accessed | tf_op | source)
XLA Modules:
  0.0 2317.9 jit_solution(3139214873398760220)
XLA Ops:
  6.5 1.3 fusion.28
  8.5 0.7 convert_element_type.3
  9.8 1.6 copy-done.5
  11.4 4.1 fusion.24
  15.5 1.9 copy-done
  17.5 0.7 dynamic-slice_select_fusion.1
  18.3 54.2 %all-gather.5.cloned.1.call-done = f32[4096,256]{1,0:T(8,128)} async-done(((f32[256,256]{1,0:T(8,128)}), f32[4096,256]{1,0:T(8,128)}) %all-gather.5.cloned.1.call-update) | async-done | bytes 4194320 | tf_op jit(solution)/shard_map/all_gather | solution.py:13
  72.5 2.5 reduce_sum.18
  75.0 8.2 fusion.30
  83.1 1.3 fusion.29
  85.3 72.4 %all-reduce.7.cloned.1.call-done = (f32[256,256]{1,0:T(8,128)}, f32[256,4096]{1,0:T(8,128)}) async-done(((f32[256,256]{1,0:T(8,128)}, f32[256,4096]{1,0:T(8,128)}), (f32[256,256]{1,0:T(8,128)}, f32[256,4096]{1,0:T(8,128)})) %all-reduce.7.cloned.1.call-update) | async-done | bytes 4456464 | tf_op jit(solution)/shard_map/psum | solution.py:85
  157.6 1.1 copy.11
  158.8 602.1 %while.62 = (s32[]{:T(128)}, f32[256,256]{1,0:T(8,128)S(1)}, f32[256,256]{0,1:T(8,128)S(1)}, s32[]{:T(128)}, s32[]{:T(128)}) while((s32[]{:T(128)}, f32[256,256]{1,0:T(8,128)S(1)}, f32[256,256]{0,1:T(8,128)S(1)}, s32[]{:T(128)}, s32[]{:T(128)}) %tuple.138), condition=%wide.region_3.4_spmd.clone, body=%wide.region_2.3_spmd.clone.sunk | while | flops 787458 | bytes 272469 | solution.py:42
  166.6 0.7 compare_select_fusion.8
  171.3 0.7 compare_select_fusion.8
  183.1 0.7 compare_select_fusion.8
  187.8 0.7 compare_select_fusion.8
  194.8 0.7 compare_select_fusion.8
  199.5 0.7 compare_select_fusion.8
  211.3 0.7 compare_select_fusion.8
  216.0 0.7 compare_select_fusion.8
  227.8 0.7 compare_select_fusion.8
  232.5 0.7 compare_select_fusion.8
  239.5 0.7 compare_select_fusion.8
  244.2 0.7 compare_select_fusion.8
  256.0 0.7 compare_select_fusion.8
  260.7 0.7 compare_select_fusion.8
  272.5 0.7 compare_select_fusion.8
  277.2 0.7 compare_select_fusion.8
  284.2 0.7 compare_select_fusion.8
  288.9 0.7 compare_select_fusion.8
  300.7 0.7 compare_select_fusion.8
  760.9 393.8 %while.63 = (s32[]{:T(128)}, f32[256,256]{1,0:T(8,128)S(1)}, f32[256,256]{1,0:T(8,128)S(1)}, s32[]{:T(128)}, s32[]{:T(128)}, /*index=5*/s32[]{:T(128)}) while((s32[]{:T(128)}, f32[256,256]{1,0:T(8,128)S(1)}, f32[256,256]{1,0:T(8,128)S(1)}, s32[]{:T(128)}, s32[]{:T(128)}, /*index=5*/s32[]{:T(128)}) %tuple.141), condition=%wide.region_5.6_spmd.clone, body=%wide.region_4.5_spmd.clone.sunk | while | flops 787459 | bytes 270449 | solution.py:56
  1154.7 5.4 fusion.31
  1160.1 3.8 fusion.32
  1164.0 3.8 convolution_subtract_fusion
  1167.8 1.9 copy-done.4
  1169.7 0.7 dynamic-slice_select_fusion
  1170.7 51.7 %all-gather.7.cloned.1.call-done = f32[4096,256]{1,0:T(8,128)} async-done(((f32[256,256]{1,0:T(8,128)}), f32[4096,256]{1,0:T(8,128)}) %all-gather.7.cloned.1.call-update) | async-done | bytes 4194320 | tf_op jit(solution)/shard_map/all_gather | solution.py:13
  1222.4 2.5 reduce_sum.19
  1224.9 8.2 fusion.34
  1233.1 1.3 fusion.33
  1234.4 73.2 %all-reduce.5.cloned.1.call-done = (f32[256,256]{1,0:T(8,128)}, f32[256,4096]{1,0:T(8,128)}) async-done(((f32[256,256]{1,0:T(8,128)}, f32[256,4096]{1,0:T(8,128)}), (f32[256,256]{1,0:T(8,128)}, f32[256,4096]{1,0:T(8,128)})) %all-reduce.5.cloned.1.call-update) | async-done | bytes 4456464 | tf_op jit(solution)/shard_map/psum | solution.py:85
  1307.6 1.1 copy.12
  1308.7 602.1 %while.64 = (s32[]{:T(128)}, f32[256,256]{1,0:T(8,128)S(1)}, f32[256,256]{0,1:T(8,128)S(1)}, s32[]{:T(128)}, s32[]{:T(128)}) while((s32[]{:T(128)}, f32[256,256]{1,0:T(8,128)S(1)}, f32[256,256]{0,1:T(8,128)S(1)}, s32[]{:T(128)}, s32[]{:T(128)}) %tuple.144), condition=%wide.region_10.11_spmd.clone, body=%wide.region_9.10_spmd.clone.sunk | while | flops 787458 | bytes 272469 | solution.py:42
  1910.8 393.8 %while.65 = (s32[]{:T(128)}, f32[256,256]{1,0:T(8,128)S(1)}, f32[256,256]{1,0:T(8,128)S(1)}, s32[]{:T(128)}, s32[]{:T(128)}, /*index=5*/s32[]{:T(128)}) while((s32[]{:T(128)}, f32[256,256]{1,0:T(8,128)S(1)}, f32[256,256]{1,0:T(8,128)S(1)}, s32[]{:T(128)}, s32[]{:T(128)}, /*index=5*/s32[]{:T(128)}) %tuple.147), condition=%wide.region_12.13_spmd.clone, body=%wide.region_11.12_spmd.clone.sunk | while | flops 787459 | bytes 270449 | solution.py:56
  2304.7 5.6 fusion.35
  2310.3 1.1 fusion.25
  (5123 shorter events, 1946.3 us)
Async XLA Ops:
  6.5 66.0 %all-gather.5.cloned.1.call-start = ((), (), s32[]{:S(2)}) async-start(), calls=%async_computation | async-start | bytes 4456448 | tf_op jit(solution)/shard_map/all_gather | solution.py:13
  9.2 2.2 copy-start.5
  15.5 2.0 copy-start
  18.2 139.4 %all-reduce.7.cloned.1.call-start = ((), (), s32[]{:S(2)}) async-start(), calls=%async_computation.3 | async-start | bytes 8912896 | tf_op jit(solution)/shard_map/psum | solution.py:85
  84.5 1138.0 %all-gather.7.cloned.1.call-start = ((), (), s32[]{:S(2)}) async-start(), calls=%async_computation.1 | async-start | bytes 4456448 | tf_op jit(solution)/shard_map/all_gather | solution.py:13
  1160.1 3.8 copy-start.2
  1160.1 3.8 copy-start.1
  1167.8 2.0 copy-start.4
  1170.5 137.1 %all-reduce.5.cloned.1.call-start = ((), (), s32[]{:S(2)}) async-start(), calls=%async_computation.2 | async-start | bytes 8912896 | tf_op jit(solution)/shard_map/psum | solution.py:85
  2304.7 5.6 copy-start.3
Sparse Core Ops, SparseCore 0:
  18.3 54.1 all-gather.4
  84.6 73.0 all-reduce.6
  1170.6 51.8 all-gather.6
  1234.5 73.0 all-reduce.4
